TPU v7x, 32 devices: a whole 2x2x4 slice. The times are simulated.
32 devices in a mesh: blk: 8 (over z, x), rep: 4 (over y, core).
Axes of the slice: x: 2, y: 2, z: 4, core: 2. Of those that a mesh axis runs over, the one named last changes fastest.
Arguments:
- features: bfloat16 [8192, 256], P(('blk', 'rep')), may hold values from -6 to 6
- weight: bfloat16 [256, 256], replicated, may hold values from -0.375 to 0.375
- pre_cot: bfloat16 [8192, 256], P(('blk', 'rep')), may hold values from -6 to 6
- tile_count: int32 [8, 4, 8], P('blk', 'rep'), may hold values from 0 to 2, as said below
- tile_rowid: int32 [8, 4, 8, 2], P('blk', 'rep'), may hold values from 0 to 3, as said below
- edge_cols: int32 [8, 4, 8, 2, 1, 256], P('blk', 'rep'), may hold values from 0 to 255
- edge_vals: bfloat16 [8, 4, 8, 2, 1, 256], P('blk', 'rep'), may hold values from -1.25 to 1.25
Outputs:
- activations: bfloat16 [8192, 256], P(('blk', 'rep'))
- grad_weight: float32 [256, 256], replicated
Inputs may be any that keep to these rules, and one draw needn't show every extreme that they name: `tile_count`: the panel p = b always has all 2 slots live. `tile_rowid`: the 2 slots of one block row, tile position and panel name distinct row tiles.
All inputs are finite; a program needn't handle non-finite values.
Results may differ from a plain program's by a relative error of at most 0.011.
Values may be sent and summed in bfloat16 or wider, within the bound.
A program may use at most 64 MiB of HBM per device.

v0:
```python
import jax
import jax.numpy as jnp
from jax import lax
from jax.sharding import PartitionSpec as P


def shifted(array, axis, by):
    count = lax.axis_size(axis)
    return lax.ppermute(array, axis, [(i, (i + by) % count) for i in range(count)])


def shards(features, weight, pre_cot, tile_count, tile_rowid, edge_cols, edge_vals):
    tile_rows = features.shape[0]
    feat_width = features.shape[1]
    rep_count = lax.axis_size("rep")
    blocks = lax.axis_size("blk")
    home_index = lax.axis_index("blk")
    counts = tile_count.reshape(-1)
    row_ids = tile_rowid.reshape(tile_rowid.shape[2], tile_rowid.shape[3])
    edge_index = edge_cols.reshape(edge_cols.shape[2:])
    edge_weight = edge_vals.reshape(edge_vals.shape[2:])
    slot_count = edge_index.shape[1]
    columns = lax.broadcasted_iota(jnp.int32, (1, 1, 1, tile_rows), 3)
    slot_ids = jnp.arange(slot_count, dtype=jnp.int32)
    zero_weight = jnp.zeros((), jnp.bfloat16)
    totals_start = jnp.zeros((rep_count * tile_rows, feat_width), jnp.float32)

    def apply_panel(totals, panel_now, panel_index):
        index_now = lax.dynamic_index_in_dim(edge_index, panel_index, 0, keepdims=False)
        weight_now = lax.dynamic_index_in_dim(edge_weight, panel_index, 0, keepdims=False)
        dense_tiles = jnp.sum(
            jnp.where(index_now[..., None] == columns, weight_now[..., None], zero_weight), axis=1
        )
        products = jnp.einsum(
            "sij,jf->sif", dense_tiles, panel_now, preferred_element_type=jnp.float32
        )
        live_mask = (slot_ids < counts[panel_index]).astype(jnp.float32)
        slot_rows = lax.dynamic_index_in_dim(row_ids, panel_index, 0, keepdims=False)
        for slot in range(slot_count):
            row_start = slot_rows[slot] * tile_rows
            current = lax.dynamic_slice_in_dim(totals, row_start, tile_rows, 0)
            totals = lax.dynamic_update_slice_in_dim(
                totals, current + products[slot] * live_mask[slot], row_start, 0
            )
        return totals

    totals = apply_panel(totals_start, features, home_index)

    def cycle_turn(turn_index, carry):
        totals_now, panel_now = carry
        panel_now = shifted(panel_now, "blk", 1)
        totals_now = apply_panel(totals_now, panel_now, (home_index - turn_index) % blocks)
        return (totals_now, panel_now)

    totals, _ = lax.fori_loop(1, blocks, cycle_turn, (totals, features))
    summed = lax.psum_scatter(totals.astype(jnp.bfloat16), "rep", scatter_dimension=0, tiled=True)
    preact = jnp.dot(summed, weight, preferred_element_type=jnp.float32)
    activations = jnp.maximum(preact, 0.0).astype(jnp.bfloat16)
    local_grad = lax.dot_general(
        summed, pre_cot, (((0,), (0,)), ((), ())), preferred_element_type=jnp.float32
    )
    total_grad = lax.psum(local_grad, ("blk", "rep"))
    node_total = blocks * rep_count * tile_rows
    grad_weight = total_grad * node_total ** (-0.5)
    return (activations, grad_weight)


def solution(mesh):
    in_specs = (
        P(("blk", "rep"), None),
        P(),
        P(("blk", "rep"), None),
        P("blk", "rep", None),
        P("blk", "rep", None, None),
        P("blk", "rep", None, None, None, None),
        P("blk", "rep", None, None, None, None),
    )
    out_specs = (P(("blk", "rep"), None), P())
    return jax.shard_map(shards, mesh=mesh, in_specs=in_specs, out_specs=out_specs, check_vma=False)
```

profile of v0, /device:TPU:0, one launch (start us, length us, event | category | flops | bytes accessed | tf_op | source)
XLA Modules:
  0.0 244.4 jit_solution(1695783370558010207)
XLA Ops:
  7.2 0.9 copy.30
  8.2 0.7 copy-done.3
  10.7 0.6 copy-done.5
  11.4 0.6 constant_dynamic-slice_fusion.3
  12.0 0.6 compare_convert_fusion.1
  12.6 0.6 fusion.37
  13.2 0.7 fusion.32
  14.3 0.6 fusion.27
  15.0 0.7 fusion.25
  15.6 67.5 %while.18 = (s32[]{:T(128)}, f32[1024,256]{1,0:T(8,128)S(1)}, bf16[256,256]{1,0:T(8,128)(2,1)S(1)}, s32[]{:T(128)}, s32[8,2]{0,1:T(2,128)S(1)}, /*index=5*/s32[8...) while((s32[]{:T(128)}, f32[1024,256]{1,0:T(8,128)S(1)}, ...), condition=%wide.region_1.2_spmd.clone, body=%wide.region_0.1_spmd.clone.sunk | while | flops 67633168 | bytes 3024392 | solution.py:55
  15.7 3.0 %collective-permute-start = (bf16[256,256]{1,0:T(8,128)(2,1)S(1)}, bf16[256,256]{1,0:T(8,128)(2,1)S(1)}, u32[]{:S(2)}, u32[]{:S(2)}) collective-permute-start(bf16[256,256]{1,0:T(8,128)(2,1)S(1)} %get-tuple-element.362), channel_id=1, source_target_pairs={{0,4},{4,8},{8,12},{12,16},{16,20},{20,24},{24,28},{28,0},{1,5},{5... | collective-permute-start | bytes 393224 | tf_op jit(solution)/shard_map/while/body/eval_jaxpr/ppermute | solution.py:9
  18.6 0.6 dynamic_slice.114
  19.3 0.7 fusion.54
  20.6 0.6 compare_convert_fusion.3
  22.4 0.6 fusion.56
  23.0 2.2 collective-permute-done
  25.5 0.6 fusion.57
  26.1 0.7 fusion.58
  26.9 0.6 dynamic_slice.114
  27.6 0.7 fusion.54
  28.9 0.6 compare_convert_fusion.3
  30.7 0.6 fusion.56
  31.3 3.3 %collective-permute-done = bf16[256,256]{1,0:T(8,128)(2,1)S(1)} collective-permute-done((bf16[256,256]{1,0:T(8,128)(2,1)S(1)}, bf16[256,256]{1,0:T(8,128)(2,1)S(1)}, u32[]{:S(2)}, u32[]{:S(2)}) %collective-permute-start) | collective-permute-done | bytes 131104 | tf_op jit(solution)/shard_map/while/body/eval_jaxpr/ppermute | solution.py:9
  34.9 0.6 fusion.57
  35.5 0.7 fusion.58
  36.3 0.6 dynamic_slice.114
  36.9 0.7 fusion.54
  38.2 0.6 compare_convert_fusion.3
  40.1 0.6 fusion.56
  40.7 3.3 %collective-permute-done = bf16[256,256]{1,0:T(8,128)(2,1)S(1)} collective-permute-done((bf16[256,256]{1,0:T(8,128)(2,1)S(1)}, bf16[256,256]{1,0:T(8,128)(2,1)S(1)}, u32[]{:S(2)}, u32[]{:S(2)}) %collective-permute-start) | collective-permute-done | bytes 131104 | tf_op jit(solution)/shard_map/while/body/eval_jaxpr/ppermute | solution.py:9
  44.3 0.6 fusion.57
  44.9 0.7 fusion.58
  45.7 0.6 dynamic_slice.114
  46.3 0.7 fusion.54
  47.6 0.6 compare_convert_fusion.3
  49.5 0.6 fusion.56
  50.1 3.3 %collective-permute-done = bf16[256,256]{1,0:T(8,128)(2,1)S(1)} collective-permute-done((bf16[256,256]{1,0:T(8,128)(2,1)S(1)}, bf16[256,256]{1,0:T(8,128)(2,1)S(1)}, u32[]{:S(2)}, u32[]{:S(2)}) %collective-permute-start) | collective-permute-done | bytes 131104 | tf_op jit(solution)/shard_map/while/body/eval_jaxpr/ppermute | solution.py:9
  53.7 0.6 fusion.57
  54.3 0.7 fusion.58
  55.1 0.6 dynamic_slice.114
  55.7 0.7 fusion.54
  57.0 0.6 compare_convert_fusion.3
  59.5 3.3 %collective-permute-done = bf16[256,256]{1,0:T(8,128)(2,1)S(1)} collective-permute-done((bf16[256,256]{1,0:T(8,128)(2,1)S(1)}, bf16[256,256]{1,0:T(8,128)(2,1)S(1)}, u32[]{:S(2)}, u32[]{:S(2)}) %collective-permute-start) | collective-permute-done | bytes 131104 | tf_op jit(solution)/shard_map/while/body/eval_jaxpr/ppermute | solution.py:9
  63.0 0.6 fusion.57
  63.7 0.7 fusion.58
  64.5 0.6 dynamic_slice.114
  65.1 0.7 fusion.54
  66.4 0.6 compare_convert_fusion.3
  68.8 3.3 %collective-permute-done = bf16[256,256]{1,0:T(8,128)(2,1)S(1)} collective-permute-done((bf16[256,256]{1,0:T(8,128)(2,1)S(1)}, bf16[256,256]{1,0:T(8,128)(2,1)S(1)}, u32[]{:S(2)}, u32[]{:S(2)}) %collective-permute-start) | collective-permute-done | bytes 131104 | tf_op jit(solution)/shard_map/while/body/eval_jaxpr/ppermute | solution.py:9
  72.4 0.6 fusion.57
  73.0 0.7 fusion.58
  73.8 0.6 dynamic_slice.114
  74.5 0.7 fusion.54
  75.8 0.6 compare_convert_fusion.3
  78.2 3.3 %collective-permute-done = bf16[256,256]{1,0:T(8,128)(2,1)S(1)} collective-permute-done((bf16[256,256]{1,0:T(8,128)(2,1)S(1)}, bf16[256,256]{1,0:T(8,128)(2,1)S(1)}, u32[]{:S(2)}, u32[]{:S(2)}) %collective-permute-start) | collective-permute-done | bytes 131104 | tf_op jit(solution)/shard_map/while/body/eval_jaxpr/ppermute | solution.py:9
  81.8 0.6 fusion.57
  82.4 0.7 fusion.58
  83.1 0.9 convert_element_type.34
  84.1 19.9 %reduce-scatter.2.cloned.1.call-done = bf16[256,256]{1,0:T(8,128)(2,1)} async-done(((bf16[1024,256]{1,0:T(8,128)(2,1)}), bf16[256,256]{1,0:T(8,128)(2,1)}) %reduce-scatter.2.cloned.1.call-update) | async-done | bytes 131088 | tf_op jit(solution)/shard_map/reduce_scatter | solution.py:56
  104.0 1.8 fusion.38
  105.8 0.9 copy-done.1
  106.8 0.8 fusion.19
  107.6 128.3 %all-reduce.2.cloned.1.call-done = f32[256,256]{1,0:T(8,128)} async-done(((f32[256,256]{1,0:T(8,128)}), f32[256,256]{1,0:T(8,128)}) %all-reduce.2.cloned.1.call-update) | async-done | bytes 262160 | tf_op jit(solution)/shard_map/psum | solution.py:62
  235.9 1.7 broadcast_multiply_fusion
  (64 shorter events, 10.0 us)
Async XLA Ops:
  7.2 96.8 %copy-start = (bf16[256,256]{1,0:T(8,128)(2,1)S(1)}, bf16[256,256]{1,0:T(8,128)(2,1)}, u32[]{:S(2)}) copy-start(bf16[256,256]{1,0:T(8,128)(2,1)} %param.11) | copy-start | bytes 393220
  7.2 96.8 %reduce-scatter.2.cloned.1.call-start = ((), (), s32[]{:S(2)}) async-start(), calls=%async_computation.1 | async-start | bytes 655360 | tf_op jit(solution)/shard_map/reduce_scatter | solution.py:56
  8.2 0.7 copy-start.3
  8.2 2.5 %copy-start.4 = (s32[1,1,8,2,1,256]{5,4,3,2,1,0:T(1,128)S(1)}, s32[1,1,8,2,1,256]{5,4,3,2,1,0:T(1,128)}, u32[]{:S(2)}) copy-start(s32[1,1,8,2,1,256]{5,4,3,2,1,0:T(1,128)} %param.14) | copy-start | bytes 49156
  10.7 0.7 copy-start.5
  15.7 9.5 %collective-permute-start = (bf16[256,256]{1,0:T(8,128)(2,1)S(1)}, bf16[256,256]{1,0:T(8,128)(2,1)S(1)}, u32[]{:S(2)}, u32[]{:S(2)}) collective-permute-start(bf16[256,256]{1,0:T(8,128)(2,1)S(1)} %get-tuple-element.362), channel_id=1, source_target_pairs={{0,4},{4,8},{8,12},{12,16},{16,20},{20,24},{24,28},{28,0},{1,5},{5... | collective-permute-start | bytes 393224 | tf_op jit(solution)/shard_map/while/body/eval_jaxpr/ppermute | solution.py:9
  26.8 7.7 %collective-permute-start = (bf16[256,256]{1,0:T(8,128)(2,1)S(1)}, bf16[256,256]{1,0:T(8,128)(2,1)S(1)}, u32[]{:S(2)}, u32[]{:S(2)}) collective-permute-start(bf16[256,256]{1,0:T(8,128)(2,1)S(1)} %get-tuple-element.362), channel_id=1, source_target_pairs={{0,4},{4,8},{8,12},{12,16},{16,20},{20,24},{24,28},{28,0},{1,5},{5... | collective-permute-start | bytes 393224 | tf_op jit(solution)/shard_map/while/body/eval_jaxpr/ppermute | solution.py:9
  36.2 7.7 %collective-permute-start = (bf16[256,256]{1,0:T(8,128)(2,1)S(1)}, bf16[256,256]{1,0:T(8,128)(2,1)S(1)}, u32[]{:S(2)}, u32[]{:S(2)}) collective-permute-start(bf16[256,256]{1,0:T(8,128)(2,1)S(1)} %get-tuple-element.362), channel_id=1, source_target_pairs={{0,4},{4,8},{8,12},{12,16},{16,20},{20,24},{24,28},{28,0},{1,5},{5... | collective-permute-start | bytes 393224 | tf_op jit(solution)/shard_map/while/body/eval_jaxpr/ppermute | solution.py:9
  45.6 7.7 %collective-permute-start = (bf16[256,256]{1,0:T(8,128)(2,1)S(1)}, bf16[256,256]{1,0:T(8,128)(2,1)S(1)}, u32[]{:S(2)}, u32[]{:S(2)}) collective-permute-start(bf16[256,256]{1,0:T(8,128)(2,1)S(1)} %get-tuple-element.362), channel_id=1, source_target_pairs={{0,4},{4,8},{8,12},{12,16},{16,20},{20,24},{24,28},{28,0},{1,5},{5... | collective-permute-start | bytes 393224 | tf_op jit(solution)/shard_map/while/body/eval_jaxpr/ppermute | solution.py:9
  55.0 7.7 %collective-permute-start = (bf16[256,256]{1,0:T(8,128)(2,1)S(1)}, bf16[256,256]{1,0:T(8,128)(2,1)S(1)}, u32[]{:S(2)}, u32[]{:S(2)}) collective-permute-start(bf16[256,256]{1,0:T(8,128)(2,1)S(1)} %get-tuple-element.362), channel_id=1, source_target_pairs={{0,4},{4,8},{8,12},{12,16},{16,20},{20,24},{24,28},{28,0},{1,5},{5... | collective-permute-start | bytes 393224 | tf_op jit(solution)/shard_map/while/body/eval_jaxpr/ppermute | solution.py:9
  64.4 7.7 %collective-permute-start = (bf16[256,256]{1,0:T(8,128)(2,1)S(1)}, bf16[256,256]{1,0:T(8,128)(2,1)S(1)}, u32[]{:S(2)}, u32[]{:S(2)}) collective-permute-start(bf16[256,256]{1,0:T(8,128)(2,1)S(1)} %get-tuple-element.362), channel_id=1, source_target_pairs={{0,4},{4,8},{8,12},{12,16},{16,20},{20,24},{24,28},{28,0},{1,5},{5... | collective-permute-start | bytes 393224 | tf_op jit(solution)/shard_map/while/body/eval_jaxpr/ppermute | solution.py:9
  73.8 7.7 %collective-permute-start = (bf16[256,256]{1,0:T(8,128)(2,1)S(1)}, bf16[256,256]{1,0:T(8,128)(2,1)S(1)}, u32[]{:S(2)}, u32[]{:S(2)}) collective-permute-start(bf16[256,256]{1,0:T(8,128)(2,1)S(1)} %get-tuple-element.362), channel_id=1, source_target_pairs={{0,4},{4,8},{8,12},{12,16},{16,20},{20,24},{24,28},{28,0},{1,5},{5... | collective-permute-start | bytes 393224 | tf_op jit(solution)/shard_map/while/body/eval_jaxpr/ppermute | solution.py:9
  84.0 151.9 %all-reduce.2.cloned.1.call-start = ((), (), s32[]{:S(2)}) async-start(), calls=%async_computation.2 | async-start | bytes 524288 | tf_op jit(solution)/shard_map/psum | solution.py:62
  105.8 0.9 copy-start.1
  105.8 1.0 copy-start.2
Sparse Core Ops, SparseCore 0:
  84.1 19.7 reduce-scatter.1
  110.9 124.9 all-reduce.1
where the time goes:
time: 245 us; the launch traced here: 244 us
  waiting for transfers between devices  170 us (69%)
  local copies, waits for them, and re-layouts  23.5 us (10%)
  other arithmetic  18 us (7%)
  between operations  15.3 us (6%)
  loops' own time  8.9 us (4%)
  matrix products  5.24 us (2%)
  starting transfers between devices  3.42 us (1%)
    psum x1, waiting for transfers between devices, shards(): total_grad = lax.psum(local_grad, ('blk', 'rep'))  128 us
    ppermute x7, waiting for transfers between devices, shifted(): lax.ppermute(array, axis, [(i, (i + by) % count) for i in range(count)])  21.7 us
    reduce_scatter x1, waiting for transfers between devices, shards(): lax.psum_scatter(totals.astype(jnp.bfloat16), 'rep', scatter_dimension=0,...  19.9 us
    dynamic_update_slice x16, other arithmetic, apply_panel(): lax.dynamic_update_slice_in_dim(totals, current + products[slot] * live_m...  10.5 us
    another operation x1, loops' own time, shards(): totals, _ = lax.fori_loop(1, blocks, cycle_turn, (totals, features))  8.9 us
    broadcast_in_dim x8, local copies, waits for them, and re-layouts, apply_panel(): jnp.where(index_now[..., None] == columns, weight_now[..., None], zero_we...  5.45 us
    convert_element_type x8, other arithmetic, apply_panel(): live_mask = (slot_ids < counts[panel_index]).astype(jnp.float32)  5.04 us
    dynamic_slice x8, local copies, waits for them, and re-layouts, apply_panel(): live_mask = (slot_ids < counts[panel_index]).astype(jnp.float32)  4.95 us
  transfers between devices with their start and end apart: 9, of which 9 were waited for; matrix products, arithmetic and copies ran while one was open for 9% of the time, Pallas kernels for 0%

commit v1 on v0

--- a/solution.py
+++ b/solution.py
@@ -59,7 +59,7 @@
     local_grad = lax.dot_general(
         summed, pre_cot, (((0,), (0,)), ((), ())), preferred_element_type=jnp.float32
     )
-    total_grad = lax.psum(local_grad, ("blk", "rep"))
+    total_grad = jnp.sum(lax.all_gather(local_grad, ("blk", "rep")), axis=0)
     node_total = blocks * rep_count * tile_rows
     grad_weight = total_grad * node_total ** (-0.5)
     return (activations, grad_weight)

time: 245 us -> 202 us (0.82)
  waiting for transfers between devices: 170 us -> 108 us
  local copies, waits for them, and re-layouts: 23.5 us -> 33.9 us
  other arithmetic: 18 us -> 21.8 us
    psum x1 -> x0, waiting for transfers between devices: 128 us -> none  [shards(): total_grad = lax.psum(local_grad, ('blk', 'rep'))]
    all_gather x0 -> x1, waiting for transfers between devices: none -> 77.8 us  [shards(): total_grad = jnp.sum(lax.all_gather(local_grad, ('blk', 'rep')), axis=0)]
    ppermute x7, waiting for transfers between devices: 21.7 us -> 9.14 us  [shifted(): lax.ppermute(array, axis, [(i, (i + by) % count) for i in range(count)])]
    dynamic_slice x8, local copies, waits for them, and re-layouts: 0.57 us -> 6 us  [apply_panel(): lax.dynamic_index_in_dim(row_ids, panel_index, 0, keepdims=False)]
    dynamic_slice x8, local copies, waits for them, and re-layouts: 4.95 us -> 10.1 us  [apply_panel(): live_mask = (slot_ids < counts[panel_index]).astype(jnp.float32)]
    reduce_sum x0 -> x1, other arithmetic: none -> 3.93 us  [shards(): total_grad = jnp.sum(lax.all_gather(local_grad, ('blk', 'rep')), axis=0)]
  transfers between devices with their start and end apart: 9 -> 9, of which waited for: 9 -> 9; matrix products, arithmetic and copies ran while one was open for 9% -> 17% of each run, Pallas kernels for 0% -> 0%
where the time goes in v1:
time: 202 us; the launch traced here: 201 us
  waiting for transfers between devices  108 us (53%)
  local copies, waits for them, and re-layouts  33.9 us (17%)
  other arithmetic  21.8 us (11%)
  between operations  15.4 us (8%)
  loops' own time  9.55 us (5%)
  matrix products  6.15 us (3%)
  starting transfers between devices  5.47 us (3%)
    all_gather x1, waiting for transfers between devices, shards(): total_grad = jnp.sum(lax.all_gather(local_grad, ('blk', 'rep')), axis=0)  77.8 us
    reduce_scatter x1, waiting for transfers between devices, shards(): lax.psum_scatter(totals.astype(jnp.bfloat16), 'rep', scatter_dimension=0,...  21.4 us
    dynamic_update_slice x16, other arithmetic, apply_panel(): lax.dynamic_update_slice_in_dim(totals, current + products[slot] * live_m...  11.2 us
    dynamic_slice x8, local copies, waits for them, and re-layouts, apply_panel(): live_mask = (slot_ids < counts[panel_index]).astype(jnp.float32)  10.1 us
    another operation x1, loops' own time, shards(): totals, _ = lax.fori_loop(1, blocks, cycle_turn, (totals, features))  9.55 us
    ppermute x7, waiting for transfers between devices, shifted(): lax.ppermute(array, axis, [(i, (i + by) % count) for i in range(count)])  9.14 us
    dynamic_slice x8, local copies, waits for them, and re-layouts, apply_panel(): lax.dynamic_index_in_dim(row_ids, panel_index, 0, keepdims=False)  6 us
    broadcast_in_dim x8, local copies, waits for them, and re-layouts, apply_panel(): jnp.where(index_now[..., None] == columns, weight_now[..., None], zero_we...  5.45 us
  transfers between devices with their start and end apart: 9, of which 9 were waited for; matrix products, arithmetic and copies ran while one was open for 17% of the time, Pallas kernels for 0%

profile of v1, /device:TPU:0, one launch (start us, length us, event | category | flops | bytes accessed | tf_op | source)
XLA Modules:
  0.0 200.7 jit_solution(1484773449566909424)
XLA Ops:
  7.2 0.9 copy.29
  8.2 0.7 constant_dynamic-slice_fusion.2
  10.7 0.7 constant_dynamic-slice_fusion.5
  11.4 0.7 copy.13
  12.2 1.3 constant_dynamic-slice_fusion.3
  14.7 0.7 fusion.32
  16.4 0.7 fusion.25
  17.1 68.3 %while.18 = (s32[]{:T(128)}, f32[1024,256]{1,0:T(8,128)S(1)}, bf16[256,256]{1,0:T(8,128)(2,1)S(1)}, s32[]{:T(128)}, s32[8,2]{0,1:T(2,128)}, /*index=5*/s32[8,2,1...) while((s32[]{:T(128)}, f32[1024,256]{1,0:T(8,128)S(1)}, ...), condition=%wide.region_1.2_spmd.clone, body=%wide.region_0.1_spmd.clone.sunk | while | flops 67633168 | bytes 3024392 | solution.py:55
  17.1 3.0 %collective-permute-start = (bf16[256,256]{1,0:T(8,128)(2,1)S(1)}, bf16[256,256]{1,0:T(8,128)(2,1)S(1)}, u32[]{:S(2)}, u32[]{:S(2)}) collective-permute-start(bf16[256,256]{1,0:T(8,128)(2,1)S(1)} %get-tuple-element.362), channel_id=1, source_target_pairs={{0,4},{4,8},{8,12},{12,16},{16,20},{20,24},{24,28},{28,0},{1,5},{5... | collective-permute-start | bytes 393224 | tf_op jit(solution)/shard_map/while/body/eval_jaxpr/ppermute | solution.py:9
  20.1 1.3 dynamic_slice.114
  21.4 0.7 fusion.54
  22.1 0.7 constant_dynamic-slice_fusion.7
  25.4 0.7 fusion.56
  27.0 0.7 fusion.57
  27.7 0.7 fusion.58
  28.4 1.0 collective-permute-start
  29.4 1.3 dynamic_slice.114
  30.7 0.7 fusion.54
  31.3 0.7 constant_dynamic-slice_fusion.7
  34.6 0.7 fusion.56
  35.3 0.9 collective-permute-done
  36.5 0.7 fusion.57
  37.2 0.7 fusion.58
  37.9 0.7 collective-permute-start
  38.6 1.3 dynamic_slice.114
  39.9 0.7 fusion.54
  40.5 0.7 constant_dynamic-slice_fusion.7
  43.8 0.7 fusion.56
  44.5 1.1 collective-permute-done
  46.0 0.7 fusion.57
  46.6 0.7 fusion.58
  47.9 1.3 dynamic_slice.114
  49.1 0.7 fusion.54
  49.8 0.7 constant_dynamic-slice_fusion.7
  53.1 0.7 fusion.56
  53.8 1.4 collective-permute-done
  55.5 0.7 fusion.57
  56.1 0.7 fusion.58
  57.1 1.3 dynamic_slice.114
  58.3 0.7 fusion.54
  59.0 0.7 constant_dynamic-slice_fusion.7
  63.0 1.6 collective-permute-done
  64.9 0.7 fusion.57
  65.6 0.7 fusion.58
  66.5 1.3 dynamic_slice.114
  67.8 0.7 fusion.54
  68.4 0.7 constant_dynamic-slice_fusion.7
  71.7 0.7 fusion.56
  72.4 1.7 collective-permute-done
  74.4 0.7 fusion.57
  75.1 0.7 fusion.58
  76.0 1.3 dynamic_slice.114
  77.3 0.7 fusion.54
  77.9 0.7 constant_dynamic-slice_fusion.7
  81.9 1.7 collective-permute-done
  83.9 0.7 fusion.57
  84.6 0.7 fusion.58
  85.4 0.9 convert_element_type.34
  86.3 21.4 %reduce-scatter.2.cloned.1.call-done = bf16[256,256]{1,0:T(8,128)(2,1)} async-done(((bf16[1024,256]{1,0:T(8,128)(2,1)}), bf16[256,256]{1,0:T(8,128)(2,1)}) %reduce-scatter.2.cloned.1.call-update) | async-done | bytes 131088 | tf_op jit(solution)/shard_map/reduce_scatter | solution.py:56
  107.8 1.8 fusion.38
  109.6 1.8 fusion.19
  111.4 77.8 %all-gather.3.cloned.1.call-done = f32[8192,256]{1,0:T(8,128)} async-done(((f32[256,256]{1,0:T(8,128)}), f32[8192,256]{1,0:T(8,128)}) %all-gather.3.cloned.1.call-update) | async-done | bytes 8388624 | tf_op jit(solution)/shard_map/all_gather | solution.py:62
  189.2 3.9 %reduce_sum.13 = f32[256,256]{1,0:T(8,128)S(1)} reduce(f32[32,256,256]{2,1,0:T(8,128)} %bitcast.78, f32[]{:T(128)} %constant.118.clone.1), dimensions={0}, to_apply=%region_3.4 | reduce | flops 2031616 | bytes 8650756 | tf_op jit(solution)/shard_map/reduce_sum | solution.py:62
  193.1 0.7 broadcast_multiply_fusion
  (57 shorter events, 16.5 us)
Async XLA Ops:
  7.2 100.6 %copy-start = (bf16[256,256]{1,0:T(8,128)(2,1)S(1)}, bf16[256,256]{1,0:T(8,128)(2,1)}, u32[]{:S(2)}) copy-start(bf16[256,256]{1,0:T(8,128)(2,1)} %param.11) | copy-start | bytes 393220
  7.2 100.6 %reduce-scatter.2.cloned.1.call-start = ((), (), s32[]{:S(2)}) async-start(), calls=%async_computation.1 | async-start | bytes 655360 | tf_op jit(solution)/shard_map/reduce_scatter | solution.py:56
  17.1 92.5 %copy-start.1 = (bf16[256,256]{1,0:T(8,128)(2,1)S(1)}, bf16[256,256]{1,0:T(8,128)(2,1)}, u32[]{:S(2)}) copy-start(bf16[256,256]{1,0:T(8,128)(2,1)} %param.10) | copy-start | bytes 393220
  17.1 9.5 %collective-permute-start = (bf16[256,256]{1,0:T(8,128)(2,1)S(1)}, bf16[256,256]{1,0:T(8,128)(2,1)S(1)}, u32[]{:S(2)}, u32[]{:S(2)}) collective-permute-start(bf16[256,256]{1,0:T(8,128)(2,1)S(1)} %get-tuple-element.362), channel_id=1, source_target_pairs={{0,4},{4,8},{8,12},{12,16},{16,20},{20,24},{24,28},{28,0},{1,5},{5... | collective-permute-start | bytes 393224 | tf_op jit(solution)/shard_map/while/body/eval_jaxpr/ppermute | solution.py:9
  28.4 7.7 %collective-permute-start = (bf16[256,256]{1,0:T(8,128)(2,1)S(1)}, bf16[256,256]{1,0:T(8,128)(2,1)S(1)}, u32[]{:S(2)}, u32[]{:S(2)}) collective-permute-start(bf16[256,256]{1,0:T(8,128)(2,1)S(1)} %get-tuple-element.362), channel_id=1, source_target_pairs={{0,4},{4,8},{8,12},{12,16},{16,20},{20,24},{24,28},{28,0},{1,5},{5... | collective-permute-start | bytes 393224 | tf_op jit(solution)/shard_map/while/body/eval_jaxpr/ppermute | solution.py:9
  37.9 7.7 %collective-permute-start = (bf16[256,256]{1,0:T(8,128)(2,1)S(1)}, bf16[256,256]{1,0:T(8,128)(2,1)S(1)}, u32[]{:S(2)}, u32[]{:S(2)}) collective-permute-start(bf16[256,256]{1,0:T(8,128)(2,1)S(1)} %get-tuple-element.362), channel_id=1, source_target_pairs={{0,4},{4,8},{8,12},{12,16},{16,20},{20,24},{24,28},{28,0},{1,5},{5... | collective-permute-start | bytes 393224 | tf_op jit(solution)/shard_map/while/body/eval_jaxpr/ppermute | solution.py:9
  47.4 7.7 %collective-permute-start = (bf16[256,256]{1,0:T(8,128)(2,1)S(1)}, bf16[256,256]{1,0:T(8,128)(2,1)S(1)}, u32[]{:S(2)}, u32[]{:S(2)}) collective-permute-start(bf16[256,256]{1,0:T(8,128)(2,1)S(1)} %get-tuple-element.362), channel_id=1, source_target_pairs={{0,4},{4,8},{8,12},{12,16},{16,20},{20,24},{24,28},{28,0},{1,5},{5... | collective-permute-start | bytes 393224 | tf_op jit(solution)/shard_map/while/body/eval_jaxpr/ppermute | solution.py:9
  56.9 7.7 %collective-permute-start = (bf16[256,256]{1,0:T(8,128)(2,1)S(1)}, bf16[256,256]{1,0:T(8,128)(2,1)S(1)}, u32[]{:S(2)}, u32[]{:S(2)}) collective-permute-start(bf16[256,256]{1,0:T(8,128)(2,1)S(1)} %get-tuple-element.362), channel_id=1, source_target_pairs={{0,4},{4,8},{8,12},{12,16},{16,20},{20,24},{24,28},{28,0},{1,5},{5... | collective-permute-start | bytes 393224 | tf_op jit(solution)/shard_map/while/body/eval_jaxpr/ppermute | solution.py:9
  66.4 7.7 %collective-permute-start = (bf16[256,256]{1,0:T(8,128)(2,1)S(1)}, bf16[256,256]{1,0:T(8,128)(2,1)S(1)}, u32[]{:S(2)}, u32[]{:S(2)}) collective-permute-start(bf16[256,256]{1,0:T(8,128)(2,1)S(1)} %get-tuple-element.362), channel_id=1, source_target_pairs={{0,4},{4,8},{8,12},{12,16},{16,20},{20,24},{24,28},{28,0},{1,5},{5... | collective-permute-start | bytes 393224 | tf_op jit(solution)/shard_map/while/body/eval_jaxpr/ppermute | solution.py:9
  75.9 7.7 %collective-permute-start = (bf16[256,256]{1,0:T(8,128)(2,1)S(1)}, bf16[256,256]{1,0:T(8,128)(2,1)S(1)}, u32[]{:S(2)}, u32[]{:S(2)}) collective-permute-start(bf16[256,256]{1,0:T(8,128)(2,1)S(1)} %get-tuple-element.362), channel_id=1, source_target_pairs={{0,4},{4,8},{8,12},{12,16},{16,20},{20,24},{24,28},{28,0},{1,5},{5... | collective-permute-start | bytes 393224 | tf_op jit(solution)/shard_map/while/body/eval_jaxpr/ppermute | solution.py:9
  86.3 102.9 %all-gather.3.cloned.1.call-start = ((), (), s32[]{:S(2)}) async-start(), calls=%async_computation.2 | async-start | bytes 8650752 | tf_op jit(solution)/shard_map/all_gather | solution.py:62
Sparse Core Ops, SparseCore 0:
  86.4 21.3 reduce-scatter.1
  111.6 77.5 all-gather.2
